TPU v7x, 32 devices: a whole 2x2x4 slice. The times are simulated.
32 devices in a mesh: grp: 2 (over y), hid: 4 (over z), ex: 4 (over x, core).
Axes of the slice: x: 2, y: 2, z: 4, core: 2. Of those that a mesh axis runs over, the one named last changes fastest.
Arguments:
- in_acts: bfloat16 [32768, 4096], P(('grp', 'ex'), 'hid'), parts along dimension 0, may hold values from -6 to 6
- out_grad: bfloat16 [32768, 14336], P(('grp', 'ex'), 'hid'), parts along dimension 0, may hold values from -6 to 6
- proj_in: bfloat16 [4096, 64], P('hid'), may hold values from -0.09375 to 0.09375
- proj_out: bfloat16 [14336, 64], P('hid'), may hold values from -0.046875 to 0.046875
- token_ids: int32 [128, 256], P(('grp', 'ex')), parts along dimension 0, may hold values from 0 to 128255
- token_weight: float32 [128256], replicated, may hold values from 0.25 to 4
- query_ids: int32 [64], P('grp'), parts along dimension 0, may hold values from 0 to 63
Outputs:
- seq_grads: float32 [128, 64, 64], P(('grp', 'ex'), 'hid'), parts along dimension 0
- scores: float32 [64, 64], P('grp', 'ex'), parts along dimension 0
There are 2 independent parts, one for each index of `grp`. A program takes and returns all parts, laid end to end along the dimension named above; an argument that names none is the same for every part. Nothing has to cross between parts.
Inputs may be any that keep to these rules, and one draw needn't show every extreme that they name: `query_ids`: indices of training sequences of this part.
All inputs are finite; a program needn't handle non-finite values.
Results may differ from a plain program's by a relative error of at most 0.0003.
Values sent between devices are 32-bit elements; how exact they have to be, the bound alone decides.
A program may use at most 128 MiB of HBM per device.

v0:
```python
import jax
import jax.numpy as jnp
from jax import lax
from jax.sharding import PartitionSpec as P


def precondition(seq_grads, fisher_in, fisher_out):
    width = seq_grads.shape[1]
    count = seq_grads.shape[0]
    trace_value = jnp.trace(fisher_in)
    identity = jnp.eye(width, dtype=jnp.float32)
    chol_in = jnp.linalg.cholesky(fisher_in + 0.1 * trace_value / width * identity)
    chol_out = jnp.linalg.cholesky(fisher_out + 0.1 * trace_value / width * identity)
    stacked = seq_grads.transpose(1, 0, 2).reshape(width, count * width)
    solved_left = jax.scipy.linalg.cho_solve((chol_out, True), stacked).reshape(width, count, width)
    turned = solved_left.transpose(2, 1, 0).reshape(width, count * width)
    solved_both = jax.scipy.linalg.cho_solve((chol_in, True), turned).reshape(width, count, width)
    return solved_both.transpose(1, 2, 0) * (trace_value / width)


def shards(in_acts, out_grad, proj_in, proj_out, token_ids, token_weight, query_ids):
    seq_count, length = token_ids.shape
    width = proj_in.shape[1]
    hid_count = lax.axis_size("hid")
    row_count = width // hid_count
    row_start = lax.axis_index("hid") * row_count
    x_part = jnp.dot(in_acts, proj_in, preferred_element_type=jnp.float32)
    weights = jnp.take(token_weight, token_ids.reshape(-1), axis=0)
    g_part = jnp.dot(out_grad, proj_out, preferred_element_type=jnp.float32) * weights[:, None]
    x_proj, g_proj = lax.psum((x_part, g_part), "hid")
    seq_grads = jnp.einsum(
        "nlr,nlc->nrc",
        g_proj.reshape(seq_count, length, width),
        x_proj.reshape(seq_count, length, width),
        precision=lax.Precision.HIGHEST,
    )
    own_rows = lax.dynamic_slice_in_dim(seq_grads, row_start, row_count, 1)
    seq_total = seq_count * lax.axis_size("ex")
    in_part = jnp.einsum("nrc,nrd->cd", seq_grads, seq_grads, precision=lax.Precision.HIGHEST)
    out_part = jnp.einsum("nrc,ndc->rd", seq_grads, seq_grads, precision=lax.Precision.HIGHEST)
    fisher_in, fisher_out = lax.psum((in_part, out_part), "ex")
    precond = precondition(seq_grads, fisher_in / seq_total, fisher_out / seq_total)
    gathered = lax.all_gather(precond, "ex", axis=0, tiled=True)
    chosen = jnp.take(gathered, query_ids, axis=0)
    scores = jnp.einsum("qrc,nrc->qn", chosen, seq_grads, precision=lax.Precision.HIGHEST)
    return (own_rows, scores)


def solution(mesh):
    placed = (
        P(("grp", "ex"), "hid"),
        P(("grp", "ex"), "hid"),
        P("hid", None),
        P("hid", None),
        P(("grp", "ex"), None),
        P(),
        P("grp"),
    )
    return jax.shard_map(
        shards,
        mesh=mesh,
        in_specs=placed,
        out_specs=(P(("grp", "ex"), "hid", None), P("grp", "ex")),
        check_vma=False,
    )
```

profile of v0, /device:TPU:0, one launch (start us, length us, event | category | flops | bytes accessed | tf_op | source)
XLA Modules:
  0.0 223.4 jit_solution(6738287502748750473)
XLA Ops:
  7.2 0.8 copy.50
  8.1 0.7 copy.49
  8.8 23.0 %gather_fusion = f32[4096]{0:T(1024)S(1)} fusion(f32[128256]{0:T(1024)S(1)} %copy-done, s32[4096]{0:T(1024)S(1)} %broadcast_clamp_fusion), kind=kCustom, calls=%fused_computation | custom fusion | bytes 49152 | tf_op jit(solution)/shard_map/jit(_take)/gather | solution.py:28
  31.9 6.1 %fusion.11 = f32[4096,64]{0,1:T(8,128)S(1)} fusion(bf16[4096,1024]{1,0:T(8,128)(2,1)} %param.10, bf16[1024,64]{0,1:T(8,128)(2,1)S(1)} %copy-done.2), kind=kOutput, calls=%fused_computation.43 | convolution fusion | flops 536870912 | bytes 9568256 | tf_op jit(solution)/shard_map/dot_general | solution.py:27
  38.0 14.2 %convolution_multiply_fusion = f32[4096,64]{0,1:T(8,128)S(1)} fusion(bf16[4096,3584]{1,0:T(8,128)(2,1)} %param.11, bf16[3584,64]{0,1:T(8,128)(2,1)S(1)} %copy-done.1, f32[4096]{0:T(1024)S(1)} %and_select_fusion), kind=kOutput, calls=%fused_computation.2 | convolution fusion | flops 1879310336 | bytes 30883840 | tf_op jit(solution)/shard_map/dot_general | solution.py:29
  52.2 1.5 copy_bitcast_fusion
  53.8 89.9 %all-reduce.4.cloned.1.call-done = (f32[16,256,64]{1,2,0:T(8,128)}, f32[16,256,64]{1,2,0:T(8,128)}) async-done(((f32[16,256,64]{1,2,0:T(8,128)}, f32[16,256,64]{1,2,0:T(8,128)}), (f32[16,256,64]{1,2,0:T(8,128)}, f32[16,256,64]{1,2,0:T(8,128)})) %all-reduce.4.cloned.1.call-update) | async-done | bytes 2097168 | tf_op jit(solution)/shard_map/psum | solution.py:30
  143.7 2.6 %fusion.12 = f32[16,64,64]{2,1,0:T(8,128)S(1)} fusion(f32[16,256,64]{1,2,0:T(8,128)} %get-tuple-element.6, f32[16,256,64]{1,2,0:T(8,128)} %get-tuple-element.7), kind=kOutput, calls=%fused_computation.44 | convolution fusion | flops 201326592 | bytes 2359296 | tf_op jit(solution)/shard_map/nlr,nlc->nrc/dot_general | solution.py:31
  146.9 1.0 convolution_bitcast_fusion.1
  147.9 12.0 %all-reduce = (f32[64,64]{0,1:T(8,128)S(1)}, f32[64,64]{0,1:T(8,128)S(1)}) all-reduce(f32[64,64]{0,1:T(8,128)S(1)} %convolution_bitcast_fusion, f32[64,64]{0,1:T(8,128)S(1)} %convolution_bitcast_fusion.1), channel_id=1, replica_groups=mesh['grp'=2,'hid'=4,'ex'=4] {'ex'}, use_global_device_ids=true, to_apply=%region_6.8 | all-reduce | flops 8192 | bytes 65536 | tf_op jit(solution)/shard_map/psum | solution.py:41
  161.3 5.8 %cholesky.44 = f32[64,64]{1,0:T(8,128)S(1)} custom-call(f32[64,64]{1,0:T(8,128)S(1)} %fusion.10), custom_call_target="Cholesky" | custom-call | tf_op jit(solution)/shard_map/jit(cholesky)/cholesky | solution.py:12
  167.2 0.6 compare_reduce_fusion.1
  167.8 0.7 fusion
  168.5 4.9 %custom-call.9 = f32[1,64,64]{1,2,0:T(8,128)S(1)} custom-call(f32[1,64,64]{2,1,0:T(8,128)S(1)} %fusion), custom_call_target="InvertDiagBlocksLowerTriangular" | custom-call | tf_op jit(solution)/shard_map/jit(_cho_solve)/triangular_solve | solution.py:17
  173.5 5.8 %cholesky.55 = f32[64,64]{1,0:T(8,128)S(1)} custom-call(f32[64,64]{1,0:T(8,128)S(1)} %fusion.6), custom_call_target="Cholesky" | custom-call | tf_op jit(solution)/shard_map/jit(cholesky)/cholesky | solution.py:13
  180.1 0.7 fusion.1
  180.7 4.9 %custom-call.8 = f32[1,64,64]{1,2,0:T(8,128)S(1)} custom-call(f32[1,64,64]{2,1,0:T(8,128)S(1)} %fusion.1), custom_call_target="InvertDiagBlocksLowerTriangular" | custom-call | tf_op jit(solution)/shard_map/jit(_cho_solve)/triangular_solve | solution.py:15
  189.0 1.0 copy.46
  190.1 1.1 copy.40
  191.1 0.7 constant_dynamic-slice_fusion
  191.8 18.9 %all-gather.2.cloned.1.call-done = f32[64,64,64]{2,1,0:T(8,128)} async-done(((f32[16,64,64]{2,1,0:T(8,128)}), f32[64,64,64]{2,1,0:T(8,128)}) %all-gather.2.cloned.1.call-update) | async-done | bytes 1048592 | tf_op jit(solution)/shard_map/all_gather | solution.py:43
  210.7 2.2 gather_fusion.1
  213.1 0.9 copy.39
  214.0 2.6 %convolution_bitcast_fusion.2 = f32[32,16]{0,1:T(8,128)} fusion(f32[32,64,64]{1,0,2:T(8,128)S(1)} %copy.39, f32[16,64,64]{1,0,2:T(8,128)} %copy.40), kind=kOutput, calls=%fused_computation.6 | convolution fusion | flops 25165824 | bytes 788480 | tf_op jit(solution)/shard_map/qrc,nrc->qn/dot_general | solution.py:45
  (39 shorter events, 5.1 us)
Async XLA Ops:
  7.2 1.6 copy-start
  7.2 136.5 %all-reduce.4.cloned.1.call-start = ((), (), s32[]{:S(2)}) async-start(), calls=%async_computation.1 | async-start | bytes 4194304 | tf_op jit(solution)/shard_map/psum | solution.py:30
  8.8 23.1 %copy-start.2 = (bf16[1024,64]{0,1:T(8,128)(2,1)S(1)}, bf16[1024,64]{0,1:T(8,128)(2,1)}, u32[]{:S(2)}) copy-start(bf16[1024,64]{0,1:T(8,128)(2,1)} %param.12) | copy-start | bytes 393220
  31.8 6.1 %copy-start.1 = (bf16[3584,64]{0,1:T(8,128)(2,1)S(1)}, bf16[3584,64]{0,1:T(8,128)(2,1)}, u32[]{:S(2)}) copy-start(bf16[3584,64]{0,1:T(8,128)(2,1)} %param.13) | copy-start | bytes 1376260
  53.7 136.3 %copy-start.3 = (s32[32]{0:T(128)S(1)}, s32[32]{0:T(128)}, u32[]{:S(2)}) copy-start(s32[32]{0:T(128)} %param.16) | copy-start | bytes 388
  53.8 156.9 %all-gather.2.cloned.1.call-start = ((), (), s32[]{:S(2)}) async-start(), calls=%async_computation | async-start | bytes 2621440 | tf_op jit(solution)/shard_map/all_gather | solution.py:43
Sparse Core Ops, SparseCore 0:
  53.9 89.7 all-reduce.3
  190.2 20.4 all-gather.1
where the time goes:
time: 224 us; the launch traced here: 223 us
  waiting for transfers between devices  109 us (49%)
  local copies, waits for them, and re-layouts  33.3 us (15%)
  matrix products  28.7 us (13%)
  other arithmetic  25 us (11%)
  between operations  15.6 us (7%)
  blocking collectives  12 us (5%)
    psum x1, waiting for transfers between devices, shards(): x_proj, g_proj = lax.psum((x_part, g_part), 'hid')  89.9 us
    gather x1, local copies, waits for them, and re-layouts, shards(): weights = jnp.take(token_weight, token_ids.reshape(-1), axis=0)  23 us
    all_gather x1, waiting for transfers between devices, shards(): gathered = lax.all_gather(precond, 'ex', axis=0, tiled=True)  18.9 us
    dot_general x1, matrix products, shards(): jnp.dot(out_grad, proj_out, preferred_element_type=jnp.float32)  14.2 us
    psum x1, blocking collectives, shards(): fisher_in, fisher_out = lax.psum((in_part, out_part), 'ex')  12 us
    another operation x3, other arithmetic, precondition(): jnp.linalg.cholesky(fisher_in + 0.1 * trace_value / width * identity)  6.52 us
    another operation x3, other arithmetic, precondition(): jnp.linalg.cholesky(fisher_out + 0.1 * trace_value / width * identity)  6.52 us
    dot_general x1, matrix products, shards(): x_part = jnp.dot(in_acts, proj_in, preferred_element_type=jnp.float32)  6.09 us
  transfers between devices with their start and end apart: 2, of which 2 were waited for; matrix products, arithmetic and copies ran while one was open for 1% of the time, Pallas kernels for 0%

commit v1 on v0

--- a/solution.py
+++ b/solution.py
@@ -1,7 +1,371 @@
+import functools
+
 import jax
 import jax.numpy as jnp
 from jax import lax
+from jax.experimental import pallas as pl
+from jax.experimental.pallas import tpu as pltpu
 from jax.sharding import PartitionSpec as P
+
+MESH = pl.DeviceIdType.MESH
+F32 = jnp.float32
+BF16 = jnp.bfloat16
+EXACT = lax.Precision.HIGHEST
+CHUNK = 128
+LAG = 3
+
+
+def contract(a, b, a_dim, b_dim, precision=EXACT):
+    return lax.dot_general(
+        a, b, (((a_dim,), (b_dim,)), ((), ())), precision=precision, preferred_element_type=F32
+    )
+
+
+def invert_pair(first, second):
+    width = first.shape[0]
+    lane = lax.broadcasted_iota(jnp.int32, (1, 2 * width), 1) % width
+    row_of = lax.broadcasted_iota(jnp.int32, (width, 2 * width), 0)
+
+    def pivot(a, j):
+        row, col = a[j : j + 1, :], a[:, j : j + 1]
+        inverse = 1.0 / a[j : j + 1, j : j + 1]
+        scaled = jnp.where(lane == j, inverse, row * inverse)
+        updated = jnp.where(lane == j, 0.0, a) - col * scaled
+        return jnp.where(row_of == j, scaled, updated)
+
+    def turn(a):
+        a = jnp.concatenate([a[8:, :], a[:8, :]], axis=0)
+        return pltpu.roll(a, 2 * width - 8, 1)
+
+    def block(_, pair):
+        a, b = pair
+        for j in range(8):
+            a, b = pivot(a, j), pivot(b, j)
+        return turn(a), turn(b)
+
+    return lax.fori_loop(0, width // 8, block, (first, second))
+
+
+def kernel(
+    hids, exs, rounds, seq_total,
+    acts, grads, proj_in, proj_out, ids, table, queries,
+    rows_out, scores_out,
+    acts_v, grads_v, proj_x, proj_g, table_v, own, came, seq, seq_flat, seq_cut, pre_cut, fish,
+    seq_all, pre_all, rows_in, partial, parts_in,
+    load_sem, hop_send, hop_recv, fish_send, fish_recv, seq_send, seq_recv,
+    row_send, row_recv, pre_send, pre_recv, part_send, part_recv,
+):
+    hid, ex = lax.axis_index("hid"), lax.axis_index("ex")
+    width = proj_in.shape[1]
+    half = rounds * CHUNK
+    owners = 2 * exs
+    mine = seq.shape[0]
+    row_count = width // hids
+    cut = width // owners
+
+    def loads(k):
+        copies = []
+        for side in range(2):
+            place = pl.ds(side * half + k * CHUNK, CHUNK)
+            land = pl.ds(k * 2 * CHUNK + side * CHUNK, CHUNK)
+            copies.append(pltpu.make_async_copy(acts.at[place], acts_v.at[land], load_sem.at[side, k]))
+            copies.append(pltpu.make_async_copy(grads.at[place], grads_v.at[land], load_sem.at[2 + side, k]))
+        return copies
+
+    def start_loads(k, _):
+        for copy in loads(k):
+            copy.start()
+        return 0
+
+    lax.fori_loop(0, rounds, start_loads, 0)
+
+    barrier = pltpu.get_barrier_semaphore()
+    for dh in range(hids):
+        for de in range(exs):
+            if dh or de:
+                pl.semaphore_signal(
+                    barrier, inc=1, device_id={"hid": (hid + dh) % hids, "ex": (ex + de) % exs}, device_id_type=MESH
+                )
+
+    proj_x[...] = jnp.concatenate([proj_in[...], jnp.zeros_like(proj_in[...])], axis=1)
+    proj_g[...] = jnp.concatenate([jnp.zeros_like(proj_out[...]), proj_out[...]], axis=1)
+    high = table[...].astype(BF16)
+    table_v[:, :128] = high
+    table_v[:, 128:] = (table[...] - high.astype(F32)).astype(BF16)
+    seq[...] = jnp.zeros_like(seq)
+    pl.semaphore_wait(barrier, hids * exs - 1)
+
+    def hop(side, k):
+        return pltpu.make_async_remote_copy(
+            src_ref=own.at[side, k],
+            dst_ref=came.at[side, k],
+            send_sem=hop_send.at[side, k],
+            recv_sem=hop_recv.at[side, k],
+            device_id={"hid": (hid + 2 * side - 1 + hids) % hids},
+            device_id_type=MESH,
+        )
+
+    def weight_row(at):
+        token = ids[pl.ds(at, 1), :]
+        row_of = lax.broadcasted_iota(jnp.int32, (table.shape[0], CHUNK), 0)
+        hot = jnp.where(row_of == token // 128, 1.0, 0.0).astype(BF16)
+        picked = contract(table_v[...], hot, 0, 0, None)
+        picked = picked[:128] + picked[128:]
+        lane_of = lax.broadcasted_iota(jnp.int32, (128, CHUNK), 0)
+        return jnp.sum(jnp.where(lane_of == token % 128, picked, 0.0), axis=0, keepdims=True)
+
+    def relay(side, r):
+        steps = side * hid + (1 - side) * (hids - 1 - hid)
+        k = r - LAG * steps
+        live = (k >= 0) & (k < rounds)
+
+        @pl.when(live & (steps > 0) & (steps < hids - 1))
+        def _():
+            hop(side, k).wait_recv()
+            own[side, k] = own[side, k] + came[side, k]
+
+        @pl.when(live & (steps < hids - 1))
+        def _():
+            hop(side, k).start()
+
+        @pl.when(live & (steps == hids - 1))
+        def _():
+            weight = weight_row(side * rounds + k)
+            hop(side, k).wait_recv()
+            both = own[side, k] + came[side, k]
+            product = contract(both.T * weight, both, 1, 0)
+            n = k * CHUNK // (half // mine)
+            seq[n] = seq[n] + product[width:, :width]
+
+    first = 1 - hid * 2 // hids
+
+    def round_of(r, _):
+        @pl.when(r < rounds)
+        def _():
+            for copy in loads(r):
+                copy.wait()
+            place = pl.ds(r * 2 * CHUNK, 2 * CHUNK)
+            both = jnp.dot(acts_v[place, :], proj_x[...], preferred_element_type=F32)
+            both = both + jnp.dot(grads_v[place, :], proj_g[...], preferred_element_type=F32)
+            own[0, r] = both[:CHUNK]
+            own[1, r] = both[CHUNK:]
+
+        relay(first, r)
+        relay(1 - first, r)
+        return 0
+
+    lax.fori_loop(0, rounds + LAG * (hids - 1), round_of, 0)
+
+    def sent(k, _):
+        for side in range(2):
+            @pl.when(hid != side * (hids - 1))
+            def _():
+                hop(side, k).wait_send()
+        return 0
+
+    lax.fori_loop(0, rounds, sent, 0)
+
+    ends = (hid == 0) | (hid == hids - 1)
+    side = hid // (hids - 1)
+    me = ex * 2 + side
+
+    def to_owner(source, target, send, recv, step, indexed):
+        other = (me + step) % owners
+        return pltpu.make_async_remote_copy(
+            src_ref=source.at[other] if indexed else source.at[me],
+            dst_ref=target.at[me],
+            send_sem=send.at[other],
+            recv_sem=recv.at[me],
+            device_id={"hid": other % 2 * (hids - 1), "ex": other // 2},
+            device_id_type=MESH,
+        )
+
+    def from_owner(target, recv, step):
+        other = (me + step) % owners
+        return pltpu.make_async_copy(target.at[other], target.at[other], recv.at[other])
+
+    def row_copy(step):
+        other = (hid + step) % hids
+        return pltpu.make_async_remote_copy(
+            src_ref=seq.at[:, pl.ds(other * row_count, row_count), :],
+            dst_ref=rows_in.at[side],
+            send_sem=row_send.at[other],
+            recv_sem=row_recv.at[side],
+            device_id={"hid": other},
+            device_id_type=MESH,
+        )
+
+    def part_copy(dh, de):
+        other_hid, other_ex = (hid + dh) % hids, (ex + de) % exs
+        return pltpu.make_async_remote_copy(
+            src_ref=partial.at[other_ex],
+            dst_ref=parts_in.at[me],
+            send_sem=part_send.at[other_hid * exs + other_ex],
+            recv_sem=part_recv.at[me],
+            device_id={"hid": other_hid, "ex": other_ex},
+            device_id_type=MESH,
+        )
+
+    others = [(dh, de) for de in range(exs) for dh in range(hids) if dh or de]
+
+    @pl.when(ends)
+    def _():
+        all_rows = seq[...].reshape(mine * width, width)
+        seq_flat[...] = all_rows
+        in_part = contract(all_rows, all_rows, 0, 0)
+        out_part = jnp.zeros((width, width), F32)
+        for n in range(mine):
+            out_part = out_part + contract(seq[n], seq[n], 1, 1)
+        fish[me] = jnp.concatenate([in_part, out_part], axis=1)
+        for step in range(1, owners):
+            to_owner(fish, fish, fish_send, fish_recv, step, False).start()
+        for n in range(mine):
+            for o in range(owners):
+                seq_cut[o, n * cut : (n + 1) * cut, :] = seq[n, o * cut : (o + 1) * cut, :]
+        seq_all[me] = seq_cut[me]
+        for step in range(1, owners):
+            to_owner(seq_cut, seq_all, seq_send, seq_recv, step, True).start()
+        for step in range(1, hids):
+            row_copy(step).start()
+        rows_in[side] = seq[:, pl.ds(hid * row_count, row_count), :]
+
+        for step in range(1, owners):
+            from_owner(fish, fish_recv, step).wait()
+        fisher = jnp.sum(fish[...], axis=0) * (1.0 / seq_total)
+        row_of = lax.broadcasted_iota(jnp.int32, (width, 2 * width), 0)
+        lane_of = lax.broadcasted_iota(jnp.int32, (width, 2 * width), 1)
+        trace = jnp.sum(jnp.where(row_of == lane_of, fisher, 0.0), axis=(0, 1), keepdims=True)
+        swapped = pltpu.roll(fisher, width, 1)
+        damp = jnp.where(row_of == lane_of % width, 0.1 * trace / width, 0.0)
+        in_inverse, out_inverse = invert_pair(
+            jnp.where(lane_of < width, fisher, swapped) + damp,
+            jnp.where(lane_of < width, swapped, fisher) + damp,
+        )
+        in_inverse = in_inverse[:, :width]
+        out_inverse = out_inverse[:, :width] * (trace / width)
+        right = contract(seq_flat[...], in_inverse, 1, 0)
+        for n in range(mine):
+            left = contract(out_inverse, right[n * width : (n + 1) * width], 1, 0)
+            for o in range(owners):
+                pre_cut[o, n * cut : (n + 1) * cut, :] = left[o * cut : (o + 1) * cut]
+        for step in range(1, owners):
+            to_owner(pre_cut, pre_all, pre_send, pre_recv, step, True).start()
+        pre_all[me] = pre_cut[me]
+        for step in range(1, owners):
+            from_owner(seq_all, seq_recv, step).wait()
+            from_owner(pre_all, pre_recv, step).wait()
+        total = owners * mine
+        gram = jnp.zeros((total, total), F32)
+        pre_flat = pre_all.reshape(total * cut, width)
+        seq_rows = seq_all.reshape(total * cut, width)
+        for row in range(cut):
+            picked = pl.ds(row, total, stride=cut)
+            gram = gram + contract(pre_flat[picked, :], seq_rows[picked, :], 1, 1)
+        hot = jnp.where(
+            lax.broadcasted_iota(jnp.int32, (total, queries.shape[1]), 0) == queries[...], 1.0, 0.0
+        )
+        chosen = contract(gram, hot, 0, 0)
+        for e in range(exs):
+            partial[e] = chosen[e * 2 * mine : (e + 1) * 2 * mine]
+        for dh, de in others:
+            part_copy(dh, de).start()
+        parts_in[me] = partial[ex]
+
+    for s in range(2):
+        @pl.when(hid != s * (hids - 1))
+        def _():
+            pltpu.make_async_copy(rows_in.at[s], rows_in.at[s], row_recv.at[s]).wait()
+    rows_out[...] = rows_in[...].reshape(rows_out.shape)
+    for o in range(owners):
+        @pl.when((hid != o % 2 * (hids - 1)) | (ex != o // 2))
+        def _():
+            pltpu.make_async_copy(parts_in.at[o], parts_in.at[o], part_recv.at[o]).wait()
+    scores_out[...] = jnp.sum(parts_in[...], axis=0)
+
+    @pl.when(ends)
+    def _():
+        for step in range(1, owners):
+            to_owner(fish, fish, fish_send, fish_recv, step, False).wait_send()
+            to_owner(seq_cut, seq_all, seq_send, seq_recv, step, True).wait_send()
+            to_owner(pre_cut, pre_all, pre_send, pre_recv, step, True).wait_send()
+        for step in range(1, hids):
+            row_copy(step).wait_send()
+        for dh, de in others:
+            part_copy(dh, de).wait_send()
+
+
+def fused(hids, exs, in_acts, out_grad, proj_in, proj_out, token_ids, token_weight, query_ids):
+    seq_count, length = token_ids.shape
+    width = proj_in.shape[1]
+    tokens, depth = in_acts.shape
+    wide = out_grad.shape[1]
+    rounds = tokens // 2 // CHUNK
+    mine = seq_count // 2
+    owners = 2 * exs
+    cut = width // owners
+    row_count = width // hids
+    count = query_ids.shape[0]
+    table_rows = -(-token_weight.shape[0] // 2048) * 16
+    table = jnp.pad(token_weight, (0, table_rows * 128 - token_weight.shape[0])).reshape(table_rows, 128)
+    vmem = pl.BlockSpec(memory_space=pltpu.VMEM)
+    whole = pl.BlockSpec(memory_space=pl.ANY)
+    sem = pltpu.SemaphoreType.DMA
+    rows, scores = pl.pallas_call(
+        functools.partial(kernel, hids, exs, rounds, seq_count * exs),
+        out_shape=(
+            jax.ShapeDtypeStruct((seq_count, row_count, width), F32),
+            jax.ShapeDtypeStruct((seq_count, count), F32),
+        ),
+        in_specs=[whole, whole] + [vmem] * 5,
+        out_specs=(vmem, vmem),
+        scratch_shapes=[
+            pltpu.VMEM((tokens, depth), BF16),
+            pltpu.VMEM((tokens, wide), BF16),
+            pltpu.VMEM((depth, 2 * width), BF16),
+            pltpu.VMEM((wide, 2 * width), BF16),
+            pltpu.VMEM((table_rows, 256), BF16),
+            pltpu.VMEM((2, rounds, CHUNK, 2 * width), F32),
+            pltpu.VMEM((2, rounds, CHUNK, 2 * width), F32),
+            pltpu.VMEM((mine, width, width), F32),
+            pltpu.VMEM((mine * width, width), F32),
+            pltpu.VMEM((owners, mine * cut, width), F32),
+            pltpu.VMEM((owners, mine * cut, width), F32),
+            pltpu.VMEM((owners, width, 2 * width), F32),
+            pltpu.VMEM((owners, mine * cut, width), F32),
+            pltpu.VMEM((owners, mine * cut, width), F32),
+            pltpu.VMEM((2, mine, row_count, width), F32),
+            pltpu.VMEM((exs, 2 * mine, count), F32),
+            pltpu.VMEM((owners, 2 * mine, count), F32),
+            sem((4, rounds)),
+            sem((2, rounds)),
+            sem((2, rounds)),
+            sem((owners,)),
+            sem((owners,)),
+            sem((owners,)),
+            sem((owners,)),
+            sem((hids,)),
+            sem((2,)),
+            sem((owners,)),
+            sem((owners,)),
+            sem((hids * exs,)),
+            sem((owners,)),
+        ],
+        compiler_params=pltpu.CompilerParams(
+            collective_id=0, has_side_effects=True, vmem_limit_bytes=60 * 1024 * 1024
+        ),
+        cost_estimate=pl.CostEstimate(
+            flops=4 * tokens * (depth + wide) * width, bytes_accessed=2 * tokens * (depth + wide), transcendentals=0
+        ),
+    )(
+        in_acts,
+        out_grad,
+        proj_in,
+        proj_out,
+        token_ids.reshape(tokens // CHUNK, CHUNK),
+        table,
+        query_ids.reshape(1, count),
+    )
+    return rows, scores.T
 
 
 def precondition(seq_grads, fisher_in, fisher_out):
@@ -47,6 +411,9 @@
 
 
 def solution(mesh):
+    hids, exs = mesh.shape["hid"], mesh.shape["ex"]
+    fits = hids > 1 and 64 % (8 * hids) == 0 and 64 % (16 * exs) == 0
+    body = functools.partial(fused, hids, exs) if fits else shards
     placed = (
         P(("grp", "ex"), "hid"),
         P(("grp", "ex"), "hid"),
@@ -57,7 +424,7 @@
         P("grp"),
     )
     return jax.shard_map(
-        shards,
+        body,
         mesh=mesh,
         in_specs=placed,
         out_specs=(P(("grp", "ex"), "hid", None), P("grp", "ex")),

time: 224 us -> 79.5 us (0.35)
  waiting for transfers between devices: 109 us -> 0 us
  Pallas kernels: 0 us -> 68.5 us
  matrix products: 28.7 us -> 0 us
  other arithmetic: 25 us -> 0 us
  local copies, waits for them, and re-layouts: 33.3 us -> 10.1 us
  between operations: 15.6 us -> 0.64 us
  blocking collectives: 12 us -> 0 us
    psum x1 -> x0, waiting for transfers between devices: 89.9 us -> none  [shards(): x_proj, g_proj = lax.psum((x_part, g_part), 'hid')]
    pallas_call x0 -> x1, Pallas kernels: none -> 68.5 us  [fused(): pl.pallas_call(functools.partial(kernel, hids, exs, rounds, seq_count * e...]
    dot_general x6 -> x0, matrix products: 27.1 us -> none  [the longest x1 14.2 us: shards(): jnp.dot(out_grad, proj_out, preferred_element_type=jnp.float32)]
    gather x2 -> x0, local copies, waits for them, and re-layouts: 25.2 us -> none  [the longest x1 23 us: shards(): weights = jnp.take(token_weight, token_ids.reshape(-1), axis=0)]
    another operation x10 -> x0, other arithmetic: 24.1 us -> none  [the longest x3 6.52 us: precondition(): jnp.linalg.cholesky(fisher_in + 0.1 * trace_value / width * identity)]
    all_gather x1 -> x0, waiting for transfers between devices: 18.9 us -> none  [shards(): gathered = lax.all_gather(precond, 'ex', axis=0, tiled=True)]
    psum x1 -> x0, blocking collectives: 12 us -> none  [shards(): fisher_in, fisher_out = lax.psum((in_part, out_part), 'ex')]
    unnamed x10 -> x4, local copies, waits for them, and re-layouts: 1.54 us -> 6.87 us
  transfers between devices with their start and end apart: 2 -> 0, of which waited for: 2 -> 0; matrix products, arithmetic and copies ran while one was open for 1% -> 0% of each run, Pallas kernels for 0% -> 0%
where the time goes in v1:
time: 79.5 us; the launch traced here: 79.2 us
  Pallas kernels  68.5 us (86%)
  local copies, waits for them, and re-layouts  10.1 us (13%)
    pallas_call x1, Pallas kernels, fused(): pl.pallas_call(functools.partial(kernel, hids, exs, rounds, seq_count * e...  68.5 us
    unnamed x4, local copies, waits for them, and re-layouts  6.87 us
    reshape x1, local copies, waits for them, and re-layouts, fused(): jnp.pad(token_weight, (0, table_rows * 128 - token_weight.shape[0]))  1.86 us

profile of v1, /device:TPU:0, one launch (start us, length us, event | category | flops | bytes accessed | tf_op | source)
XLA Modules:
  0.0 79.2 jit_solution(2125528218912016544)
XLA Ops:
  0.6 1.3 %reshape.13.ids = s32[32,128]{1,0:T(8,128)} reshape(s32[16,256]{1,0:T(8,128)} %param.11) | data formatting | bytes 32768 | tf_op jit(solution)/shard_map/reshape | solution.py:364
  2.0 1.7 %copy.9.proj_in = bf16[1024,64]{1,0:T(8,128)(2,1)} copy(bf16[1024,64]{0,1:T(8,128)(2,1)} %param.9) | data formatting | bytes 262144 | tf_op args[2]
  3.7 1.9 %pad_bitcast_fusion.table = f32[1008,128]{1,0:T(8,128)} fusion(f32[128256]{0:T(1024)} %param.12), kind=kLoop, calls=%fused_computation | loop fusion | bytes 1029120 | tf_op jit(solution)/shard_map/reshape | solution.py:309
  5.6 2.3 %copy.10.proj_out = bf16[3584,64]{1,0:T(8,128)(2,1)} copy(bf16[3584,64]{0,1:T(8,128)(2,1)} %param.10) | data formatting | bytes 917504 | tf_op args[3]
  7.8 68.5 %shard_map.86 = (f32[16,16,64]{2,1,0:T(8,128)}, f32[16,32]{1,0:T(8,128)}) custom-call(bf16[4096,1024]{1,0:T(8,128)(2,1)} %acts.1, bf16[4096,3584]{1,0:T(8,128)(2,1)} %grads.1, bf16[1024,64]{1,0:T(8,128)(2,1)} %copy.9.proj_in, bf16[3584,64]{1,0:T(8,128)(2,1)} %copy.10.proj_out, s32[32,128]{1,0:T(8,128)} %reshape.13.ids, f32[1008,128]{1,0:T(8,128)} %pad_bitcast_fusion.table, ...), custom_call_target="tpu_custom_call" | custom-call | flops 4831838208 | bytes 37748736 | tf_op jit(solution)/shard_map/pallas_call | solution.py:313
  76.3 1.6 %copy.13 = f32[16,16,64]{2,1,0:T(8,128)} copy(f32[16,16,64]{2,1,0:T(8,128)} %get-tuple-element.8) | data formatting | bytes 131072
  77.9 1.3 %copy.14 = f32[32,16]{0,1:T(8,128)} copy(f32[32,16]{0,1:T(8,128)} %bitcast.4) | data formatting | bytes 4096

commit v2 on v1

--- a/solution.py
+++ b/solution.py
@@ -13,6 +13,7 @@
 EXACT = lax.Precision.HIGHEST
 CHUNK = 128
 LAG = 3
+AHEAD = 3
 
 
 def contract(a, b, a_dim, b_dim, precision=EXACT):
@@ -48,20 +49,28 @@
 
 def kernel(
     hids, exs, rounds, seq_total,
-    acts, grads, proj_in, proj_out, ids, table, queries,
+    acts, grads, proj_in_hbm, proj_out_hbm, ids, table_hbm, queries,
     rows_out, scores_out,
-    acts_v, grads_v, proj_x, proj_g, table_v, own, came, seq, seq_flat, seq_cut, pre_cut, fish,
+    acts_v, grads_v, proj_in, proj_out, table, table_v, own, came, seq, seq_cut, pre_cut, fish,
     seq_all, pre_all, rows_in, partial, parts_in,
-    load_sem, hop_send, hop_recv, fish_send, fish_recv, seq_send, seq_recv,
+    small_sem, load_sem, hop_send, hop_recv, fish_send, fish_recv, seq_send, seq_recv,
     row_send, row_recv, pre_send, pre_recv, part_send, part_recv,
 ):
     hid, ex = lax.axis_index("hid"), lax.axis_index("ex")
-    width = proj_in.shape[1]
+    width = proj_in.shape[0]
     half = rounds * CHUNK
     owners = 2 * exs
     mine = seq.shape[0]
     row_count = width // hids
     cut = width // owners
+    ends = (hid == 0) | (hid == hids - 1)
+    side = hid // (hids - 1)
+    me = ex * 2 + side
+
+    small = [
+        pltpu.make_async_copy(source, target, small_sem.at[i])
+        for i, (source, target) in enumerate(((proj_in_hbm, proj_in), (proj_out_hbm, proj_out), (table_hbm, table)))
+    ]
 
     def loads(k):
         copies = []
@@ -77,8 +86,6 @@
             copy.start()
         return 0
 
-    lax.fori_loop(0, rounds, start_loads, 0)
-
     barrier = pltpu.get_barrier_semaphore()
     for dh in range(hids):
         for de in range(exs):
@@ -87,12 +94,16 @@
                     barrier, inc=1, device_id={"hid": (hid + dh) % hids, "ex": (ex + de) % exs}, device_id_type=MESH
                 )
 
-    proj_x[...] = jnp.concatenate([proj_in[...], jnp.zeros_like(proj_in[...])], axis=1)
-    proj_g[...] = jnp.concatenate([jnp.zeros_like(proj_out[...]), proj_out[...]], axis=1)
+    for copy in small:
+        copy.start()
+    lax.fori_loop(0, min(AHEAD, rounds), start_loads, 0)
+    for copy in small:
+        copy.wait()
     high = table[...].astype(BF16)
     table_v[:, :128] = high
     table_v[:, 128:] = (table[...] - high.astype(F32)).astype(BF16)
     seq[...] = jnp.zeros_like(seq)
+    fish[me] = jnp.zeros((width, 2 * width), F32)
     pl.semaphore_wait(barrier, hids * exs - 1)
 
     def hop(side, k):
@@ -105,8 +116,12 @@
             device_id_type=MESH,
         )
 
-    def weight_row(at):
-        token = ids[pl.ds(at, 1), :]
+    def weight_row(side, k):
+        per_seq = ids.shape[1] // CHUNK
+        row = ids[pl.ds(side * mine + k // per_seq, 1), :]
+        token = row[:, :CHUNK]
+        for piece in range(1, per_seq):
+            token = jnp.where(k % per_seq == piece, row[:, piece * CHUNK : (piece + 1) * CHUNK], token)
         row_of = lax.broadcasted_iota(jnp.int32, (table.shape[0], CHUNK), 0)
         hot = jnp.where(row_of == token // 128, 1.0, 0.0).astype(BF16)
         picked = contract(table_v[...], hot, 0, 0, None)
@@ -130,12 +145,20 @@
 
         @pl.when(live & (steps == hids - 1))
         def _():
-            weight = weight_row(side * rounds + k)
+            weight = weight_row(side, k)
             hop(side, k).wait_recv()
             both = own[side, k] + came[side, k]
-            product = contract(both.T * weight, both, 1, 0)
-            n = k * CHUNK // (half // mine)
-            seq[n] = seq[n] + product[width:, :width]
+            per_seq = ids.shape[1] // CHUNK
+            n = k // per_seq
+            seq[n] = seq[n] + contract(both[width:] * weight, both[:width], 1, 1)
+
+            @pl.when(k % per_seq == per_seq - 1)
+            def _():
+                done = seq[n]
+                sides = [contract(done, done, 0, 0), contract(done, done, 1, 1)]
+                fish[me] = fish[me] + jnp.concatenate(sides, axis=1)
+                for o in range(owners):
+                    seq_cut[o, pl.ds(pl.multiple_of(n * cut, cut), cut), :] = done[o * cut : (o + 1) * cut]
 
     first = 1 - hid * 2 // hids
 
@@ -144,11 +167,17 @@
         def _():
             for copy in loads(r):
                 copy.wait()
+
+            @pl.when(r + AHEAD < rounds)
+            def _():
+                start_loads(r + AHEAD, 0)
+
             place = pl.ds(r * 2 * CHUNK, 2 * CHUNK)
-            both = jnp.dot(acts_v[place, :], proj_x[...], preferred_element_type=F32)
-            both = both + jnp.dot(grads_v[place, :], proj_g[...], preferred_element_type=F32)
-            own[0, r] = both[:CHUNK]
-            own[1, r] = both[CHUNK:]
+            x_part = contract(proj_in[...], acts_v[place, :], 1, 1, None)
+            g_part = contract(proj_out[...], grads_v[place, :], 1, 1, None)
+            for side in range(2):
+                own[side, r, :width] = x_part[:, side * CHUNK : (side + 1) * CHUNK]
+                own[side, r, width:] = g_part[:, side * CHUNK : (side + 1) * CHUNK]
 
         relay(first, r)
         relay(1 - first, r)
@@ -163,11 +192,6 @@
                 hop(side, k).wait_send()
         return 0
 
-    lax.fori_loop(0, rounds, sent, 0)
-
-    ends = (hid == 0) | (hid == hids - 1)
-    side = hid // (hids - 1)
-    me = ex * 2 + side
 
     def to_owner(source, target, send, recv, step, indexed):
         other = (me + step) % owners
@@ -206,31 +230,22 @@
             device_id_type=MESH,
         )
 
-    others = [(dh, de) for de in range(exs) for dh in range(hids) if dh or de]
+    others = [(dh, de) for dh in range(hids - 1, -1, -1) for de in range(exs) if dh or de]
+    partners = [*range(1, owners, 2), *range(2, owners, 2)]
 
     @pl.when(ends)
     def _():
-        all_rows = seq[...].reshape(mine * width, width)
-        seq_flat[...] = all_rows
-        in_part = contract(all_rows, all_rows, 0, 0)
-        out_part = jnp.zeros((width, width), F32)
-        for n in range(mine):
-            out_part = out_part + contract(seq[n], seq[n], 1, 1)
-        fish[me] = jnp.concatenate([in_part, out_part], axis=1)
-        for step in range(1, owners):
+        for step in partners:
             to_owner(fish, fish, fish_send, fish_recv, step, False).start()
-        for n in range(mine):
-            for o in range(owners):
-                seq_cut[o, n * cut : (n + 1) * cut, :] = seq[n, o * cut : (o + 1) * cut, :]
+        for step in partners:
+            from_owner(fish, fish_recv, step).wait()
         seq_all[me] = seq_cut[me]
-        for step in range(1, owners):
+        for step in partners:
             to_owner(seq_cut, seq_all, seq_send, seq_recv, step, True).start()
         for step in range(1, hids):
             row_copy(step).start()
         rows_in[side] = seq[:, pl.ds(hid * row_count, row_count), :]
 
-        for step in range(1, owners):
-            from_owner(fish, fish_recv, step).wait()
         fisher = jnp.sum(fish[...], axis=0) * (1.0 / seq_total)
         row_of = lax.broadcasted_iota(jnp.int32, (width, 2 * width), 0)
         lane_of = lax.broadcasted_iota(jnp.int32, (width, 2 * width), 1)
@@ -243,15 +258,15 @@
         )
         in_inverse = in_inverse[:, :width]
         out_inverse = out_inverse[:, :width] * (trace / width)
-        right = contract(seq_flat[...], in_inverse, 1, 0)
+        right = contract(seq[...].reshape(mine * width, width), in_inverse, 1, 0)
         for n in range(mine):
             left = contract(out_inverse, right[n * width : (n + 1) * width], 1, 0)
             for o in range(owners):
                 pre_cut[o, n * cut : (n + 1) * cut, :] = left[o * cut : (o + 1) * cut]
-        for step in range(1, owners):
+        for step in partners:
             to_owner(pre_cut, pre_all, pre_send, pre_recv, step, True).start()
         pre_all[me] = pre_cut[me]
-        for step in range(1, owners):
+        for step in partners:
             from_owner(seq_all, seq_recv, step).wait()
             from_owner(pre_all, pre_recv, step).wait()
         total = owners * mine
@@ -282,6 +297,8 @@
             pltpu.make_async_copy(parts_in.at[o], parts_in.at[o], part_recv.at[o]).wait()
     scores_out[...] = jnp.sum(parts_in[...], axis=0)
 
+    lax.fori_loop(0, rounds, sent, 0)
+
     @pl.when(ends)
     def _():
         for step in range(1, owners):
@@ -305,8 +322,7 @@
     cut = width // owners
     row_count = width // hids
     count = query_ids.shape[0]
-    table_rows = -(-token_weight.shape[0] // 2048) * 16
-    table = jnp.pad(token_weight, (0, table_rows * 128 - token_weight.shape[0])).reshape(table_rows, 128)
+    table_rows = token_weight.shape[0] // 128
     vmem = pl.BlockSpec(memory_space=pltpu.VMEM)
     whole = pl.BlockSpec(memory_space=pl.ANY)
     sem = pltpu.SemaphoreType.DMA
@@ -316,18 +332,18 @@
             jax.ShapeDtypeStruct((seq_count, row_count, width), F32),
             jax.ShapeDtypeStruct((seq_count, count), F32),
         ),
-        in_specs=[whole, whole] + [vmem] * 5,
+        in_specs=[whole, whole, whole, whole, vmem, whole, vmem],
         out_specs=(vmem, vmem),
         scratch_shapes=[
             pltpu.VMEM((tokens, depth), BF16),
             pltpu.VMEM((tokens, wide), BF16),
-            pltpu.VMEM((depth, 2 * width), BF16),
-            pltpu.VMEM((wide, 2 * width), BF16),
+            pltpu.VMEM((width, depth), BF16),
+            pltpu.VMEM((width, wide), BF16),
+            pltpu.VMEM((table_rows, 128), F32),
             pltpu.VMEM((table_rows, 256), BF16),
-            pltpu.VMEM((2, rounds, CHUNK, 2 * width), F32),
-            pltpu.VMEM((2, rounds, CHUNK, 2 * width), F32),
+            pltpu.VMEM((2, rounds, 2 * width, CHUNK), F32),
+            pltpu.VMEM((2, rounds, 2 * width, CHUNK), F32),
             pltpu.VMEM((mine, width, width), F32),
-            pltpu.VMEM((mine * width, width), F32),
             pltpu.VMEM((owners, mine * cut, width), F32),
             pltpu.VMEM((owners, mine * cut, width), F32),
             pltpu.VMEM((owners, width, 2 * width), F32),
@@ -336,6 +352,7 @@
             pltpu.VMEM((2, mine, row_count, width), F32),
             pltpu.VMEM((exs, 2 * mine, count), F32),
             pltpu.VMEM((owners, 2 * mine, count), F32),
+            sem((3,)),
             sem((4, rounds)),
             sem((2, rounds)),
             sem((2, rounds)),
@@ -359,10 +376,10 @@
     )(
         in_acts,
         out_grad,
-        proj_in,
-        proj_out,
-        token_ids.reshape(tokens // CHUNK, CHUNK),
-        table,
+        proj_in.T,
+        proj_out.T,
+        token_ids,
+        token_weight.reshape(table_rows, 128),
         query_ids.reshape(1, count),
     )
     return rows, scores.T

time: 79.5 us -> 70.6 us (0.89)
  local copies, waits for them, and re-layouts: 10.1 us -> 2.86 us
  Pallas kernels: 68.5 us -> 66.7 us
    unnamed x4 -> x2, local copies, waits for them, and re-layouts: 6.87 us -> 2.86 us
    reshape x2 -> x0, local copies, waits for them, and re-layouts: 3.19 us -> none  [the longest x1 1.86 us: fused(): jnp.pad(token_weight, (0, table_rows * 128 - token_weight.shape[0]))]
    pallas_call x1, Pallas kernels: 68.5 us -> 66.7 us  [fused(): pl.pallas_call(functools.partial(kernel, hids, exs, rounds, seq_count * e...]
where the time goes in v2:
time: 70.6 us; the launch traced here: 70.2 us
  Pallas kernels  66.7 us (94%)
  local copies, waits for them, and re-layouts  2.86 us (4%)
    pallas_call x1, Pallas kernels, fused(): pl.pallas_call(functools.partial(kernel, hids, exs, rounds, seq_count * e...  66.7 us
    unnamed x2, local copies, waits for them, and re-layouts  2.86 us

profile of v2, /device:TPU:0, one launch (start us, length us, event | category | flops | bytes accessed | tf_op | source)
XLA Modules:
  0.0 70.2 jit_solution(16578733621938628923)
XLA Ops:
  0.6 66.7 %shard_map.86 = (f32[16,16,64]{2,1,0:T(8,128)}, f32[16,32]{1,0:T(8,128)}) custom-call(bf16[4096,1024]{1,0:T(8,128)(2,1)} %acts.1, bf16[4096,3584]{1,0:T(8,128)(2,1)} %grads.1, bf16[64,1024]{1,0:T(8,128)(2,1)} %bitcast.7, bf16[64,3584]{1,0:T(8,128)(2,1)} %bitcast.6, s32[16,256]{1,0:T(8,128)} %ids.1, f32[1002,128]{1,0:T(8,128)} %bitcast.5, s32[1,32]{1,0:T(1,128)} %bitcast.9), custom_call_target="tpu_custom_call" | custom-call | flops 4831838208 | bytes 37748736 | tf_op jit(solution)/shard_map/pallas_call | solution.py:329
  67.4 1.6 %copy.11 = f32[16,16,64]{2,1,0:T(8,128)} copy(f32[16,16,64]{2,1,0:T(8,128)} %get-tuple-element.8) | data formatting | bytes 131072
  68.9 1.3 %copy.12 = f32[32,16]{0,1:T(8,128)} copy(f32[32,16]{0,1:T(8,128)} %bitcast.8) | data formatting | bytes 4096

commit v3 on v2

--- a/solution.py
+++ b/solution.py
@@ -13,6 +13,7 @@
 EXACT = lax.Precision.HIGHEST
 CHUNK = 128
 LAG = 3
+LATE = 4
 AHEAD = 3
 
 
@@ -131,7 +132,7 @@
 
     def relay(side, r):
         steps = side * hid + (1 - side) * (hids - 1 - hid)
-        k = r - LAG * steps
+        k = r - LAG * steps - LATE * (steps // (hids - 1))
         live = (k >= 0) & (k < rounds)
 
         @pl.when(live & (steps > 0) & (steps < hids - 1))
@@ -183,7 +184,7 @@
         relay(1 - first, r)
         return 0
 
-    lax.fori_loop(0, rounds + LAG * (hids - 1), round_of, 0)
+    lax.fori_loop(0, rounds + LAG * (hids - 1) + LATE, round_of, 0)
 
     def sent(k, _):
         for side in range(2):
@@ -290,12 +291,12 @@
         @pl.when(hid != s * (hids - 1))
         def _():
             pltpu.make_async_copy(rows_in.at[s], rows_in.at[s], row_recv.at[s]).wait()
-    rows_out[...] = rows_in[...].reshape(rows_out.shape)
+    rows_out[...] = rows_in[...]
     for o in range(owners):
         @pl.when((hid != o % 2 * (hids - 1)) | (ex != o // 2))
         def _():
             pltpu.make_async_copy(parts_in.at[o], parts_in.at[o], part_recv.at[o]).wait()
-    scores_out[...] = jnp.sum(parts_in[...], axis=0)
+    scores_out[...] = parts_in[...]
 
     lax.fori_loop(0, rounds, sent, 0)
 
@@ -309,6 +310,11 @@
             row_copy(step).wait_send()
         for dh, de in others:
             part_copy(dh, de).wait_send()
+
+
+def finish(rows, parts, rows_out, scores_out):
+    rows_out[...] = rows[...].reshape(rows_out.shape)
+    scores_out[...] = jnp.sum(parts[...], axis=0).T
 
 
 def fused(hids, exs, in_acts, out_grad, proj_in, proj_out, token_ids, token_weight, query_ids):
@@ -326,11 +332,11 @@
     vmem = pl.BlockSpec(memory_space=pltpu.VMEM)
     whole = pl.BlockSpec(memory_space=pl.ANY)
     sem = pltpu.SemaphoreType.DMA
-    rows, scores = pl.pallas_call(
+    rows, parts = pl.pallas_call(
         functools.partial(kernel, hids, exs, rounds, seq_count * exs),
         out_shape=(
-            jax.ShapeDtypeStruct((seq_count, row_count, width), F32),
-            jax.ShapeDtypeStruct((seq_count, count), F32),
+            jax.ShapeDtypeStruct((2, mine, row_count, width), F32),
+            jax.ShapeDtypeStruct((owners, seq_count, count), F32),
         ),
         in_specs=[whole, whole, whole, whole, vmem, whole, vmem],
         out_specs=(vmem, vmem),
@@ -382,7 +388,15 @@
         token_weight.reshape(table_rows, 128),
         query_ids.reshape(1, count),
     )
-    return rows, scores.T
+    return pl.pallas_call(
+        finish,
+        out_shape=(
+            jax.ShapeDtypeStruct((seq_count, row_count, width), F32),
+            jax.ShapeDtypeStruct((count, seq_count), F32),
+        ),
+        in_specs=[vmem, vmem],
+        out_specs=(vmem, vmem),
+    )(rows, parts)
 
 
 def precondition(seq_grads, fisher_in, fisher_out):

time: 70.6 us -> 70.7 us (level)
  Pallas kernels: 66.7 us -> 68.3 us
  local copies, waits for them, and re-layouts: 2.86 us -> 1.38 us
    unnamed x2 -> x0, local copies, waits for them, and re-layouts: 2.86 us -> none
    pallas_call x0 -> x1, Pallas kernels: none -> 1.6 us  [fused(): pl.pallas_call(finish, out_shape=(jax.ShapeDtypeStruct((seq_count, row_co...]
    pallas_call x0 -> x1, local copies, waits for them, and re-layouts: none -> 1.38 us  [fused(): pl.pallas_call(finish, out_shape=(jax.ShapeDtypeStruct((seq_count, row_co...]
where the time goes in v3:
time: 70.7 us; the launch traced here: 70.4 us
  Pallas kernels  68.3 us (97%)
  local copies, waits for them, and re-layouts  1.38 us (2%)
    pallas_call x1, Pallas kernels, fused(): pl.pallas_call(functools.partial(kernel, hids, exs, rounds, seq_count * e...  66.7 us
    pallas_call x1, Pallas kernels, fused(): pl.pallas_call(finish, out_shape=(jax.ShapeDtypeStruct((seq_count, row_co...  1.6 us

profile of v3, /device:TPU:0, one launch (start us, length us, event | category | flops | bytes accessed | tf_op | source)
XLA Modules:
  0.0 70.4 jit_solution(17326327236643053696)
XLA Ops:
  0.6 66.7 %shard_map.86 = (f32[2,8,16,64]{3,2,1,0:T(8,128)}, f32[8,16,32]{2,1,0:T(8,128)}) custom-call(bf16[4096,1024]{1,0:T(8,128)(2,1)} %acts.1, bf16[4096,3584]{1,0:T(8,128)(2,1)} %grads.1, bf16[64,1024]{1,0:T(8,128)(2,1)} %bitcast.6, bf16[64,3584]{1,0:T(8,128)(2,1)} %bitcast.5, s32[16,256]{1,0:T(8,128)} %ids.1, f32[1002,128]{1,0:T(8,128)} %bitcast.4, s32[1,32]{1,0:T(1,128)} %bitcast.7), custom_call_target="tpu_custom_call" | custom-call | flops 4831838208 | bytes 37748736 | tf_op jit(solution)/shard_map/pallas_call | solution.py:335
  67.4 1.6 %shard_map.87 = (f32[16,16,64]{2,1,0:T(8,128)}, f32[32,16]{1,0:T(8,128)}) custom-call(f32[2,8,16,64]{3,2,1,0:T(8,128)} %get-tuple-element.4.rows, f32[8,16,32]{2,1,0:T(8,128)} %get-tuple-element.5.parts), custom_call_target="tpu_custom_call" | custom-call | tf_op jit(solution)/shard_map/pallas_call | solution.py:391
  69.0 1.4 %copy.9 = f32[32,16]{0,1:T(8,128)} copy(f32[32,16]{1,0:T(8,128)} %get-tuple-element.7) | data formatting | bytes 4096 | tf_op jit(solution)/shard_map/pallas_call | solution.py:391
